TPU v7x, 32 devices: a whole 2x2x4 slice. The times are simulated.
32 devices in a mesh: dp: 4 (over z), ctx: 8 (over y, x, core).
Axes of the slice: x: 2, y: 2, z: 4, core: 2. Of those that a mesh axis runs over, the one named last changes fastest.
Arguments:
- queries: bfloat16 [4096, 4096], P(('dp', 'ctx')), parts along dimension 0, may hold values from -0.6640625 to 0.6640625
- key_vectors: bfloat16 [4096, 4096], P(('dp', 'ctx')), parts along dimension 0, may hold values from -0.6640625 to 0.6640625
- values: bfloat16 [4096, 4096], P(('dp', 'ctx')), parts along dimension 0, may hold values from -0.6640625 to 0.6640625
- out_grad: bfloat16 [4096, 4096], P(('dp', 'ctx')), parts along dimension 0, may hold values from -0.6640625 to 0.6640625
- log_decay: bfloat16 [4096, 32], P(('dp', 'ctx')), parts along dimension 0, may hold values from -2.2 to 0
Outputs:
- attended: bfloat16 [4096, 4096], P(('dp', 'ctx')), parts along dimension 0
- query_grad: bfloat16 [4096, 4096], P(('dp', 'ctx')), parts along dimension 0
- key_grad: bfloat16 [4096, 4096], P(('dp', 'ctx')), parts along dimension 0
- value_grad: bfloat16 [4096, 4096], P(('dp', 'ctx')), parts along dimension 0
There are 4 independent parts, one for each index of `dp`. A program takes and returns all parts, laid end to end along the dimension named above; each array names one. Nothing has to cross between parts.
All inputs are finite; a program needn't handle non-finite values.
Results may differ from a plain program's by a relative error of at most 0.001.
Values may be sent and summed in bfloat16 or wider, within the bound.
A program may use at most 320 MiB of HBM per device.

v0:
```python
import functools

import jax
import jax.numpy as jnp
from jax import lax
from jax.experimental import pallas as pl
from jax.experimental.pallas import tpu as pltpu
from jax.sharding import PartitionSpec as P

MESH = pl.DeviceIdType.MESH
HEADS_PER_CHUNK = 2


def mm(a, b, ca, cb):
    return lax.dot_general(
        a, b, (((ca,), (cb,)), ((), ())), preferred_element_type=jnp.float32
    )


def split(x):
    high = x.astype(jnp.bfloat16)
    return high, (x - high.astype(jnp.float32)).astype(jnp.bfloat16)


def kernel(
    n, per, q_ref, k_ref, v_ref, g_ref, ld_ref, att_ref, dq_ref, dk_ref, dv_ref,
    fin, fout, bin_, bout, ecum, erest, etot, att0, dq0, dk0, dv0,
    fsend, frecv, bsend, brecv,
):
    me = lax.axis_index("ctx")
    up, down = lax.rem(me + 1, n), lax.rem(me + n - 1, n)
    tokens, heads = ld_ref.shape
    width = q_ref.shape[1] // heads
    chunks = heads // per
    bf16 = jnp.bfloat16

    barrier = pltpu.get_barrier_semaphore()

    @pl.when(me > 0)
    def _():
        pl.semaphore_signal(barrier, inc=1, device_id={"ctx": down}, device_id_type=MESH)

    @pl.when(me < n - 1)
    def _():
        pl.semaphore_signal(barrier, inc=1, device_id={"ctx": up}, device_id_type=MESH)

    pl.semaphore_wait(barrier, jnp.minimum(me, 1) + jnp.minimum(n - 1 - me, 1))

    @pl.when(me == 0)
    def _():
        fin[...] = jnp.zeros_like(fin)

    @pl.when(me == n - 1)
    def _():
        bin_[...] = jnp.zeros_like(bin_)

    row = lax.broadcasted_iota(jnp.int32, (tokens, tokens), 0)
    col = lax.broadcasted_iota(jnp.int32, (tokens, tokens), 1)
    causal = row >= col
    lower = jnp.where(causal, 1.0, 0.0).astype(bf16)
    upper = jnp.where(row < col, 1.0, 0.0).astype(bf16)
    head_row = lax.broadcasted_iota(jnp.int32, (heads, width), 0)

    def columns(h):
        return pl.ds(pl.multiple_of(h * width, width), width)

    def steps(h):
        pick = jnp.where(head_row == h, 1.0, 0.0).astype(bf16)
        return mm(ld_ref[...], pick, 1, 0)

    def forward_copy(c):
        part = pl.ds(c * per, per)
        return pltpu.make_async_remote_copy(
            src_ref=fout.at[part], dst_ref=fin.at[part],
            send_sem=fsend.at[c], recv_sem=frecv.at[c],
            device_id={"ctx": up}, device_id_type=MESH,
        )

    def backward_copy(c):
        part = pl.ds(c * per, per)
        return pltpu.make_async_remote_copy(
            src_ref=bout.at[part], dst_ref=bin_.at[part],
            send_sem=bsend.at[c], recv_sem=brecv.at[c],
            device_id={"ctx": down}, device_id_type=MESH,
        )

    def states(c):
        for j in range(per):
            h = c * per + j
            cols = columns(h)
            step = steps(h).astype(bf16)
            cum = mm(lower, step, 1, 0)
            ec = jnp.exp(cum)
            er = jnp.exp(mm(upper, step, 1, 0))
            ecum[h] = ec
            erest[h] = er
            etot[h] = jnp.broadcast_to(ec[tokens - 1 :, :], etot.shape[1:])
            kh, kl = split(k_ref[:, cols].astype(jnp.float32) * er)
            v = v_ref[:, cols]
            fout[h] = mm(kh, v, 0, 0) + mm(kl, v, 0, 0)
            qh, ql = split(q_ref[:, cols].astype(jnp.float32) * ec)
            g = g_ref[:, cols]
            bout[h] = mm(qh, g, 0, 0) + mm(ql, g, 0, 0)

    def forward(c):
        @pl.when(me > 0)
        def _():
            forward_copy(c).wait_recv()

        @pl.when(me < n - 1)
        def _():
            for j in range(per):
                h = c * per + j
                fout[h] = fout[h] + etot[h][:1, :] * fin[h]
            forward_copy(c).start()

    def backward(c):
        @pl.when(me < n - 1)
        def _():
            backward_copy(c).wait_recv()

        @pl.when(me > 0)
        def _():
            for j in range(per):
                h = c * per + j
                bout[h] = bout[h] + etot[h][:1, :] * bin_[h]
            backward_copy(c).start()

    def intra(c):
        for j in range(per):
            h = c * per + j
            cols = columns(h)
            q, k, v, g = q_ref[:, cols], k_ref[:, cols], v_ref[:, cols], g_ref[:, cols]
            between = jnp.where(row > col, steps(h), 0.0).astype(bf16)
            weights = jnp.where(causal, jnp.exp(mm(lower, between, 1, 0)), 0.0)
            sh, sl = split(mm(q, k, 1, 1) * weights)
            th, tl = split(mm(g, v, 1, 1) * weights)
            att0[:, cols] = mm(sh, v, 1, 0) + mm(sl, v, 1, 0)
            dq0[:, cols] = mm(th, k, 1, 0) + mm(tl, k, 1, 0)
            dk0[:, cols] = mm(th, q, 0, 0) + mm(tl, q, 0, 0)
            dv0[:, cols] = mm(sh, g, 0, 0) + mm(sl, g, 0, 0)

    def cross(c):
        for j in range(per):
            h = c * per + j
            cols = columns(h)
            q, k, v, g = q_ref[:, cols], k_ref[:, cols], v_ref[:, cols], g_ref[:, cols]
            ec, er = ecum[h], erest[h]
            ph, pl_ = split(fin[h])
            nh, nl = split(bin_[h])
            att_ref[:, cols] = (
                att0[:, cols] + ec * (mm(q, ph, 1, 0) + mm(q, pl_, 1, 0))
            ).astype(bf16)
            dq_ref[:, cols] = (
                dq0[:, cols] + ec * (mm(g, ph, 1, 1) + mm(g, pl_, 1, 1))
            ).astype(bf16)
            dk_ref[:, cols] = (
                dk0[:, cols] + er * (mm(v, nh, 1, 1) + mm(v, nl, 1, 1))
            ).astype(bf16)
            dv_ref[:, cols] = (
                dv0[:, cols] + er * (mm(k, nh, 1, 0) + mm(k, nl, 1, 0))
            ).astype(bf16)

    def guarded(c, work):
        @pl.when((c >= 0) & (c < chunks))
        def _():
            work(c)

    def tick(t, carry):
        guarded(t, states)
        guarded(t - me, forward)
        guarded(t - (n - 1 - me), backward)
        guarded(t, intra)
        guarded(t - jnp.maximum(me, n - 1 - me), cross)
        return carry

    lax.fori_loop(0, chunks + n - 1, tick, 0)

    def drain(c, carry):
        @pl.when(me < n - 1)
        def _():
            forward_copy(c).wait_send()

        @pl.when(me > 0)
        def _():
            backward_copy(c).wait_send()

        return carry

    lax.fori_loop(0, chunks, drain, 0)


def solution(mesh):
    n = mesh.shape["ctx"]

    def shards(queries, key_vectors, values, out_grad, log_decay):
        tokens, heads = log_decay.shape
        total = queries.shape[1]
        width = total // heads
        per = HEADS_PER_CHUNK
        chunks = heads // per
        f32 = jnp.float32
        vmem = pl.BlockSpec(memory_space=pltpu.VMEM)
        state = pltpu.VMEM((heads, width, width), f32)
        decay = pltpu.VMEM((heads, tokens, width), f32)
        rows = pltpu.VMEM((tokens, total), f32)
        sems = pltpu.SemaphoreType.DMA((chunks,))
        return pl.pallas_call(
            functools.partial(kernel, n, per),
            out_shape=[jax.ShapeDtypeStruct((tokens, total), jnp.bfloat16)] * 4,
            in_specs=[vmem] * 5,
            out_specs=[vmem] * 4,
            scratch_shapes=[state] * 4
            + [decay] * 2
            + [pltpu.VMEM((heads, 8, width), f32)]
            + [rows] * 4
            + [sems] * 4,
            compiler_params=pltpu.CompilerParams(
                collective_id=0, has_side_effects=True, vmem_limit_bytes=48 * 1024 * 1024
            ),
        )(queries, key_vectors, values, out_grad, log_decay)

    spec = P(("dp", "ctx"), None)
    return jax.shard_map(
        shards, mesh=mesh, in_specs=(spec,) * 5, out_specs=(spec,) * 4, check_vma=False
    )
```

profile of v0, /device:TPU:0, one launch (start us, length us, event | category | flops | bytes accessed | tf_op | source)
XLA Modules:
  0.0 86.8 jit_solution(5925765797216693411)
XLA Ops:
  0.6 0.8 copy.9.ld_ref
  1.4 0.0 copy-start
  1.4 1.2 %copy-done = bf16[128,4096]{1,0:T(8,128)(2,1)S(1)} copy-done((bf16[128,4096]{1,0:T(8,128)(2,1)S(1)}, bf16[128,4096]{1,0:T(8,128)(2,1)}, u32[]{:S(2)}) %copy-start) | copy-done | bytes 1048600
  2.7 80.2 %shard_map.84 = (bf16[128,4096]{1,0:T(8,128)(2,1)S(1)}, bf16[128,4096]{1,0:T(8,128)(2,1)S(1)}, bf16[128,4096]{1,0:T(8,128)(2,1)S(1)}, bf16[128,4096]{1,0:T(8,128)(2,1)S(1)}) custom-call(bf16[128,4096]{1,0:T(8,128)(2,1)S(1)} %copy-done, bf16[128,4096]{1,0:T(8,128)(2,1)} %k_ref.1, bf16[128,4096]{1,0:T(8,128)(2,1)} %v_ref.1, bf16[128,4096]{1,0:T(8,128)(2,1)} %g_ref.1, ...), custom_call_target="tpu_custom_call" | custom-call | tf_op jit(solution)/shard_map/pallas_call | solution.py:208
  82.9 1.0 %copy.14 = bf16[128,4096]{1,0:T(8,128)(2,1)} copy(bf16[128,4096]{1,0:T(8,128)(2,1)S(1)} %get-tuple-element.8) | data formatting | bytes 2097152
  83.8 1.0 %copy.15 = bf16[128,4096]{1,0:T(8,128)(2,1)} copy(bf16[128,4096]{1,0:T(8,128)(2,1)S(1)} %get-tuple-element.9) | data formatting | bytes 2097152
  84.8 1.0 %copy.16 = bf16[128,4096]{1,0:T(8,128)(2,1)} copy(bf16[128,4096]{1,0:T(8,128)(2,1)S(1)} %get-tuple-element.10) | data formatting | bytes 2097152
  85.8 1.0 %copy.17 = bf16[128,4096]{1,0:T(8,128)(2,1)} copy(bf16[128,4096]{1,0:T(8,128)(2,1)S(1)} %get-tuple-element.11) | data formatting | bytes 2097152
Async XLA Ops:
  1.4 1.2 %copy-start = (bf16[128,4096]{1,0:T(8,128)(2,1)S(1)}, bf16[128,4096]{1,0:T(8,128)(2,1)}, u32[]{:S(2)}) copy-start(bf16[128,4096]{1,0:T(8,128)(2,1)} %q_ref.1) | copy-start | bytes 3145732
where the time goes:
time: 87 us; the launch traced here: 86.8 us
  Pallas kernels  80.2 us (92%)
  local copies, waits for them, and re-layouts  5.92 us (7%)
    pallas_call x1, Pallas kernels, shards(): pl.pallas_call(functools.partial(kernel, n, per), out_shape=[jax.ShapeDty...  80.2 us
    unnamed x7, local copies, waits for them, and re-layouts  5.92 us

commit v1 on v0

--- a/solution.py
+++ b/solution.py
@@ -9,6 +9,7 @@
 
 MESH = pl.DeviceIdType.MESH
 HEADS_PER_CHUNK = 2
+LAG = 2
 
 
 def mm(a, b, ca, cb):
@@ -22,9 +23,13 @@
     return high, (x - high.astype(jnp.float32)).astype(jnp.bfloat16)
 
 
+def pair(parts, axis):
+    return jnp.concatenate(parts, axis=axis)
+
+
 def kernel(
     n, per, q_ref, k_ref, v_ref, g_ref, ld_ref, att_ref, dq_ref, dk_ref, dv_ref,
-    fin, fout, bin_, bout, ecum, erest, etot, att0, dq0, dk0, dv0,
+    fin, fout, bin_, bout, ecum, erest, weights, etot, att0, dq0, dk0, dv0,
     fsend, frecv, bsend, brecv,
 ):
     me = lax.axis_index("ctx")
@@ -46,14 +51,6 @@
 
     pl.semaphore_wait(barrier, jnp.minimum(me, 1) + jnp.minimum(n - 1 - me, 1))
 
-    @pl.when(me == 0)
-    def _():
-        fin[...] = jnp.zeros_like(fin)
-
-    @pl.when(me == n - 1)
-    def _():
-        bin_[...] = jnp.zeros_like(bin_)
-
     row = lax.broadcasted_iota(jnp.int32, (tokens, tokens), 0)
     col = lax.broadcasted_iota(jnp.int32, (tokens, tokens), 1)
     causal = row >= col
@@ -88,21 +85,28 @@
         for j in range(per):
             h = c * per + j
             cols = columns(h)
-            step = steps(h).astype(bf16)
-            cum = mm(lower, step, 1, 0)
-            ec = jnp.exp(cum)
+            step = steps(h)
+            between = jnp.where(row > col, step, 0.0).astype(bf16)
+            step = step.astype(bf16)
+            sums = mm(lower, pair([step, between], 1), 1, 0)
+            ec = jnp.exp(sums[:, :width])
             er = jnp.exp(mm(upper, step, 1, 0))
             ecum[h] = ec
             erest[h] = er
             etot[h] = jnp.broadcast_to(ec[tokens - 1 :, :], etot.shape[1:])
-            kh, kl = split(k_ref[:, cols].astype(jnp.float32) * er)
-            v = v_ref[:, cols]
-            fout[h] = mm(kh, v, 0, 0) + mm(kl, v, 0, 0)
-            qh, ql = split(q_ref[:, cols].astype(jnp.float32) * ec)
-            g = g_ref[:, cols]
-            bout[h] = mm(qh, g, 0, 0) + mm(ql, g, 0, 0)
+            weights[h] = jnp.where(causal, jnp.exp(sums[:, width:]), 0.0)
+            v, g = v_ref[:, cols], g_ref[:, cols]
+            k_scaled = k_ref[:, cols].astype(jnp.float32) * er
+            fout[h] = mm(pair(split(k_scaled), 0), pair([v, v], 0), 0, 0)
+            q_scaled = q_ref[:, cols].astype(jnp.float32) * ec
+            bout[h] = mm(pair(split(q_scaled), 0), pair([g, g], 0), 0, 0)
 
     def forward(c):
+        @pl.when(me == 0)
+        def _():
+            for j in range(per):
+                fin[c * per + j] = jnp.zeros((width, width), jnp.float32)
+
         @pl.when(me > 0)
         def _():
             forward_copy(c).wait_recv()
@@ -115,6 +119,11 @@
             forward_copy(c).start()
 
     def backward(c):
+        @pl.when(me == n - 1)
+        def _():
+            for j in range(per):
+                bin_[c * per + j] = jnp.zeros((width, width), jnp.float32)
+
         @pl.when(me < n - 1)
         def _():
             backward_copy(c).wait_recv()
@@ -131,14 +140,13 @@
             h = c * per + j
             cols = columns(h)
             q, k, v, g = q_ref[:, cols], k_ref[:, cols], v_ref[:, cols], g_ref[:, cols]
-            between = jnp.where(row > col, steps(h), 0.0).astype(bf16)
-            weights = jnp.where(causal, jnp.exp(mm(lower, between, 1, 0)), 0.0)
-            sh, sl = split(mm(q, k, 1, 1) * weights)
-            th, tl = split(mm(g, v, 1, 1) * weights)
-            att0[:, cols] = mm(sh, v, 1, 0) + mm(sl, v, 1, 0)
-            dq0[:, cols] = mm(th, k, 1, 0) + mm(tl, k, 1, 0)
-            dk0[:, cols] = mm(th, q, 0, 0) + mm(tl, q, 0, 0)
-            dv0[:, cols] = mm(sh, g, 0, 0) + mm(sl, g, 0, 0)
+            weight = weights[h]
+            scores = split(mm(q, k, 1, 1) * weight)
+            grad_scores = split(mm(g, v, 1, 1) * weight)
+            att0[:, cols] = mm(pair(scores, 1), pair([v, v], 0), 1, 0)
+            dq0[:, cols] = mm(pair(grad_scores, 1), pair([k, k], 0), 1, 0)
+            dk0[:, cols] = mm(pair(grad_scores, 0), pair([q, q], 0), 0, 0)
+            dv0[:, cols] = mm(pair(scores, 0), pair([g, g], 0), 0, 0)
 
     def cross(c):
         for j in range(per):
@@ -146,20 +154,15 @@
             cols = columns(h)
             q, k, v, g = q_ref[:, cols], k_ref[:, cols], v_ref[:, cols], g_ref[:, cols]
             ec, er = ecum[h], erest[h]
-            ph, pl_ = split(fin[h])
-            nh, nl = split(bin_[h])
-            att_ref[:, cols] = (
-                att0[:, cols] + ec * (mm(q, ph, 1, 0) + mm(q, pl_, 1, 0))
-            ).astype(bf16)
-            dq_ref[:, cols] = (
-                dq0[:, cols] + ec * (mm(g, ph, 1, 1) + mm(g, pl_, 1, 1))
-            ).astype(bf16)
-            dk_ref[:, cols] = (
-                dk0[:, cols] + er * (mm(v, nh, 1, 1) + mm(v, nl, 1, 1))
-            ).astype(bf16)
-            dv_ref[:, cols] = (
-                dv0[:, cols] + er * (mm(k, nh, 1, 0) + mm(k, nl, 1, 0))
-            ).astype(bf16)
+            before, after = split(fin[h]), split(bin_[h])
+            att = mm(pair([q, q], 1), pair(before, 0), 1, 0)
+            att_ref[:, cols] = (att0[:, cols] + ec * att).astype(bf16)
+            dq = mm(pair([g, g], 1), pair(before, 1), 1, 1)
+            dq_ref[:, cols] = (dq0[:, cols] + ec * dq).astype(bf16)
+            dk = mm(pair([v, v], 1), pair(after, 1), 1, 1)
+            dk_ref[:, cols] = (dk0[:, cols] + er * dk).astype(bf16)
+            dv = mm(pair([k, k], 1), pair(after, 0), 1, 0)
+            dv_ref[:, cols] = (dv0[:, cols] + er * dv).astype(bf16)
 
     def guarded(c, work):
         @pl.when((c >= 0) & (c < chunks))
@@ -168,13 +171,13 @@
 
     def tick(t, carry):
         guarded(t, states)
-        guarded(t - me, forward)
-        guarded(t - (n - 1 - me), backward)
+        guarded(t - LAG * me, forward)
+        guarded(t - LAG * (n - 1 - me), backward)
         guarded(t, intra)
-        guarded(t - jnp.maximum(me, n - 1 - me), cross)
+        guarded(t - LAG * jnp.maximum(me, n - 1 - me), cross)
         return carry
 
-    lax.fori_loop(0, chunks + n - 1, tick, 0)
+    lax.fori_loop(0, chunks + LAG * (n - 1), tick, 0)
 
     def drain(c, carry):
         @pl.when(me < n - 1)
@@ -211,7 +214,7 @@
             in_specs=[vmem] * 5,
             out_specs=[vmem] * 4,
             scratch_shapes=[state] * 4
-            + [decay] * 2
+            + [decay] * 3
             + [pltpu.VMEM((heads, 8, width), f32)]
             + [rows] * 4
             + [sems] * 4,

time: 87 us -> 73.9 us (0.85)
  Pallas kernels: 80.2 us -> 67.1 us
    pallas_call x1, Pallas kernels: 80.2 us -> 67.1 us  [shards(): pl.pallas_call(functools.partial(kernel, n, per), out_shape=[jax.ShapeDty...]
where the time goes in v1:
time: 73.9 us; the launch traced here: 73.7 us
  Pallas kernels  67.1 us (91%)
  local copies, waits for them, and re-layouts  5.92 us (8%)
    pallas_call x1, Pallas kernels, shards(): pl.pallas_call(functools.partial(kernel, n, per), out_shape=[jax.ShapeDty...  67.1 us
    unnamed x7, local copies, waits for them, and re-layouts  5.92 us

profile of v1, /device:TPU:0, one launch (start us, length us, event | category | flops | bytes accessed | tf_op | source)
XLA Modules:
  0.0 73.7 jit_solution(16668976257620581969)
XLA Ops:
  0.6 0.8 %copy.9.ld_ref = bf16[128,32]{1,0:T(8,128)(2,1)S(1)} copy(bf16[128,32]{0,1:T(8,128)(2,1)} %param.9) | data formatting | bytes 16384 | tf_op args[4]
  1.4 0.0 copy-start
  1.4 1.2 %copy-done = bf16[128,4096]{1,0:T(8,128)(2,1)S(1)} copy-done((bf16[128,4096]{1,0:T(8,128)(2,1)S(1)}, bf16[128,4096]{1,0:T(8,128)(2,1)}, u32[]{:S(2)}) %copy-start) | copy-done | bytes 1048600
  2.7 67.1 %shard_map.84 = (bf16[128,4096]{1,0:T(8,128)(2,1)S(1)}, bf16[128,4096]{1,0:T(8,128)(2,1)S(1)}, bf16[128,4096]{1,0:T(8,128)(2,1)S(1)}, bf16[128,4096]{1,0:T(8,128)(2,1)S(1)}) custom-call(bf16[128,4096]{1,0:T(8,128)(2,1)S(1)} %copy-done, bf16[128,4096]{1,0:T(8,128)(2,1)} %k_ref.1, bf16[128,4096]{1,0:T(8,128)(2,1)} %v_ref.1, bf16[128,4096]{1,0:T(8,128)(2,1)} %g_ref.1, ...), custom_call_target="tpu_custom_call" | custom-call | tf_op jit(solution)/shard_map/pallas_call | solution.py:211
  69.8 1.0 %copy.14 = bf16[128,4096]{1,0:T(8,128)(2,1)} copy(bf16[128,4096]{1,0:T(8,128)(2,1)S(1)} %get-tuple-element.8) | data formatting | bytes 2097152
  70.8 1.0 %copy.15 = bf16[128,4096]{1,0:T(8,128)(2,1)} copy(bf16[128,4096]{1,0:T(8,128)(2,1)S(1)} %get-tuple-element.9) | data formatting | bytes 2097152
  71.8 1.0 %copy.16 = bf16[128,4096]{1,0:T(8,128)(2,1)} copy(bf16[128,4096]{1,0:T(8,128)(2,1)S(1)} %get-tuple-element.10) | data formatting | bytes 2097152
  72.7 1.0 %copy.17 = bf16[128,4096]{1,0:T(8,128)(2,1)} copy(bf16[128,4096]{1,0:T(8,128)(2,1)S(1)} %get-tuple-element.11) | data formatting | bytes 2097152
Async XLA Ops:
  1.4 1.2 %copy-start = (bf16[128,4096]{1,0:T(8,128)(2,1)S(1)}, bf16[128,4096]{1,0:T(8,128)(2,1)}, u32[]{:S(2)}) copy-start(bf16[128,4096]{1,0:T(8,128)(2,1)} %q_ref.1) | copy-start | bytes 3145732

commit v2 on v1

--- a/solution.py
+++ b/solution.py
@@ -10,6 +10,7 @@
 MESH = pl.DeviceIdType.MESH
 HEADS_PER_CHUNK = 2
 LAG = 2
+GROUPS = 4
 
 
 def mm(a, b, ca, cb):
@@ -28,16 +29,31 @@
 
 
 def kernel(
-    n, per, q_ref, k_ref, v_ref, g_ref, ld_ref, att_ref, dq_ref, dk_ref, dv_ref,
-    fin, fout, bin_, bout, ecum, erest, weights, etot, att0, dq0, dk0, dv0,
-    fsend, frecv, bsend, brecv,
+    n, per, q_hbm, k_hbm, v_hbm, g_hbm, ld_ref, att_ref, dq_ref, dk_ref, dv_ref,
+    q_ref, k_ref, v_ref, g_ref, fin, fout, bin_, bout, ecum, erest, weights, etot, att0, dq0, dk0, dv0,
+    fsend, frecv, bsend, brecv, loaded,
 ):
     me = lax.axis_index("ctx")
     up, down = lax.rem(me + 1, n), lax.rem(me + n - 1, n)
     tokens, heads = ld_ref.shape
-    width = q_ref.shape[1] // heads
+    width = q_hbm.shape[1] // heads
     chunks = heads // per
     bf16 = jnp.bfloat16
+
+    span = heads * width // GROUPS
+    chunks_per_group = chunks // GROUPS
+
+    def loads(group):
+        cols = pl.ds(pl.multiple_of(group * span, span), span)
+        arrays = ((q_hbm, q_ref), (k_hbm, k_ref), (v_hbm, v_ref), (g_hbm, g_ref))
+        return [
+            pltpu.make_async_copy(src.at[:, cols], dst.at[:, cols], loaded.at[i, group])
+            for i, (src, dst) in enumerate(arrays)
+        ]
+
+    for group in range(GROUPS):
+        for load in loads(group):
+            load.start()
 
     barrier = pltpu.get_barrier_semaphore()
 
@@ -80,6 +96,12 @@
             send_sem=bsend.at[c], recv_sem=brecv.at[c],
             device_id={"ctx": down}, device_id_type=MESH,
         )
+
+    def arrive(c):
+        @pl.when(lax.rem(c, chunks_per_group) == 0)
+        def _():
+            for load in loads(lax.div(c, chunks_per_group)):
+                load.wait()
 
     def states(c):
         for j in range(per):
@@ -170,6 +192,7 @@
             work(c)
 
     def tick(t, carry):
+        guarded(t, arrive)
         guarded(t, states)
         guarded(t - LAG * me, forward)
         guarded(t - LAG * (n - 1 - me), backward)
@@ -211,13 +234,15 @@
         return pl.pallas_call(
             functools.partial(kernel, n, per),
             out_shape=[jax.ShapeDtypeStruct((tokens, total), jnp.bfloat16)] * 4,
-            in_specs=[vmem] * 5,
+            in_specs=[pl.BlockSpec(memory_space=pltpu.HBM)] * 4 + [vmem],
             out_specs=[vmem] * 4,
-            scratch_shapes=[state] * 4
+            scratch_shapes=[pltpu.VMEM((tokens, total), jnp.bfloat16)] * 4
+            + [state] * 4
             + [decay] * 3
             + [pltpu.VMEM((heads, 8, width), f32)]
             + [rows] * 4
-            + [sems] * 4,
+            + [sems] * 4
+            + [pltpu.SemaphoreType.DMA((4, GROUPS))],
             compiler_params=pltpu.CompilerParams(
                 collective_id=0, has_side_effects=True, vmem_limit_bytes=48 * 1024 * 1024
             ),

time: 73.9 us -> 71.5 us (0.968)
  Pallas kernels: 67.1 us -> 64.7 us
    pallas_call x1, Pallas kernels: 67.1 us -> 64.7 us  [shards(): pl.pallas_call(functools.partial(kernel, n, per), out_shape=[jax.ShapeDty...]
where the time goes in v2:
time: 71.5 us; the launch traced here: 71.3 us
  Pallas kernels  64.7 us (90%)
  local copies, waits for them, and re-layouts  5.92 us (8%)
    pallas_call x1, Pallas kernels, shards(): pl.pallas_call(functools.partial(kernel, n, per), out_shape=[jax.ShapeDty...  64.7 us
    unnamed x7, local copies, waits for them, and re-layouts  5.92 us

profile of v2, /device:TPU:0, one launch (start us, length us, event | category | flops | bytes accessed | tf_op | source)
XLA Modules:
  0.0 71.3 jit_solution(2823383309468710389)
XLA Ops:
  0.6 0.8 %copy.9.ld_ref = bf16[128,32]{1,0:T(8,128)(2,1)S(1)} copy(bf16[128,32]{0,1:T(8,128)(2,1)} %param.9) | data formatting | bytes 16384 | tf_op args[4]
  1.4 0.0 copy-start
  1.4 1.2 %copy-done = bf16[128,4096]{1,0:T(8,128)(2,1)S(1)} copy-done((bf16[128,4096]{1,0:T(8,128)(2,1)S(1)}, bf16[128,4096]{1,0:T(8,128)(2,1)}, u32[]{:S(2)}) %copy-start) | copy-done | bytes 1048600
  2.7 64.7 %shard_map.84 = (bf16[128,4096]{1,0:T(8,128)(2,1)S(1)}, bf16[128,4096]{1,0:T(8,128)(2,1)S(1)}, bf16[128,4096]{1,0:T(8,128)(2,1)S(1)}, bf16[128,4096]{1,0:T(8,128)(2,1)S(1)}) custom-call(bf16[128,4096]{1,0:T(8,128)(2,1)S(1)} %copy-done, bf16[128,4096]{1,0:T(8,128)(2,1)} %k_hbm.1, bf16[128,4096]{1,0:T(8,128)(2,1)} %v_hbm.1, bf16[128,4096]{1,0:T(8,128)(2,1)} %g_hbm.1, ...), custom_call_target="tpu_custom_call" | custom-call | tf_op jit(solution)/shard_map/pallas_call | solution.py:234
  67.4 1.0 %copy.14 = bf16[128,4096]{1,0:T(8,128)(2,1)} copy(bf16[128,4096]{1,0:T(8,128)(2,1)S(1)} %get-tuple-element.8) | data formatting | bytes 2097152
  68.4 1.0 %copy.15 = bf16[128,4096]{1,0:T(8,128)(2,1)} copy(bf16[128,4096]{1,0:T(8,128)(2,1)S(1)} %get-tuple-element.9) | data formatting | bytes 2097152
  69.3 1.0 %copy.16 = bf16[128,4096]{1,0:T(8,128)(2,1)} copy(bf16[128,4096]{1,0:T(8,128)(2,1)S(1)} %get-tuple-element.10) | data formatting | bytes 2097152
  70.3 1.0 %copy.17 = bf16[128,4096]{1,0:T(8,128)(2,1)} copy(bf16[128,4096]{1,0:T(8,128)(2,1)S(1)} %get-tuple-element.11) | data formatting | bytes 2097152
Async XLA Ops:
  1.4 1.2 %copy-start = (bf16[128,4096]{1,0:T(8,128)(2,1)S(1)}, bf16[128,4096]{1,0:T(8,128)(2,1)}, u32[]{:S(2)}) copy-start(bf16[128,4096]{1,0:T(8,128)(2,1)} %q_hbm.1) | copy-start | bytes 3145732

commit v3 on v2

--- a/solution.py
+++ b/solution.py
@@ -191,16 +191,33 @@
         def _():
             work(c)
 
+    def local(c):
+        states(c)
+        intra(c)
+
     def tick(t, carry):
+        guarded(t - 1 - LAG * me, forward)
+        guarded(t - 1 - LAG * (n - 1 - me), backward)
         guarded(t, arrive)
-        guarded(t, states)
-        guarded(t - LAG * me, forward)
-        guarded(t - LAG * (n - 1 - me), backward)
-        guarded(t, intra)
-        guarded(t - LAG * jnp.maximum(me, n - 1 - me), cross)
+        late = t - 1 - LAG * jnp.maximum(me, n - 1 - me)
+        crossing = (late >= 0) & (late < chunks)
+
+        @pl.when((t < chunks) & crossing)
+        def _():
+            local(t)
+            cross(late)
+
+        @pl.when((t < chunks) & ((late < 0) | (late >= chunks)))
+        def _():
+            local(t)
+
+        @pl.when((t >= chunks) & crossing)
+        def _():
+            cross(late)
+
         return carry
 
-    lax.fori_loop(0, chunks + LAG * (n - 1), tick, 0)
+    lax.fori_loop(0, chunks + LAG * (n - 1) + 1, tick, 0)
 
     def drain(c, carry):
         @pl.when(me < n - 1)

time: 71.5 us -> 70.8 us (level)
    pallas_call x1, Pallas kernels: 64.7 us -> 64 us  [shards(): pl.pallas_call(functools.partial(kernel, n, per), out_shape=[jax.ShapeDty...]
where the time goes in v3:
time: 70.8 us; the launch traced here: 70.6 us
  Pallas kernels  64 us (90%)
  local copies, waits for them, and re-layouts  5.92 us (8%)
    pallas_call x1, Pallas kernels, shards(): pl.pallas_call(functools.partial(kernel, n, per), out_shape=[jax.ShapeDty...  64 us
    unnamed x7, local copies, waits for them, and re-layouts  5.92 us

profile of v3, /device:TPU:0, one launch (start us, length us, event | category | flops | bytes accessed | tf_op | source)
XLA Modules:
  0.0 70.6 jit_solution(12364344592803442091)
XLA Ops:
  0.6 0.8 %copy.9.ld_ref = bf16[128,32]{1,0:T(8,128)(2,1)S(1)} copy(bf16[128,32]{0,1:T(8,128)(2,1)} %param.9) | data formatting | bytes 16384 | tf_op args[4]
  1.4 0.0 copy-start
  1.4 1.2 %copy-done = bf16[128,4096]{1,0:T(8,128)(2,1)S(1)} copy-done((bf16[128,4096]{1,0:T(8,128)(2,1)S(1)}, bf16[128,4096]{1,0:T(8,128)(2,1)}, u32[]{:S(2)}) %copy-start) | copy-done | bytes 1048600
  2.7 64.0 %shard_map.84 = (bf16[128,4096]{1,0:T(8,128)(2,1)S(1)}, bf16[128,4096]{1,0:T(8,128)(2,1)S(1)}, bf16[128,4096]{1,0:T(8,128)(2,1)S(1)}, bf16[128,4096]{1,0:T(8,128)(2,1)S(1)}) custom-call(bf16[128,4096]{1,0:T(8,128)(2,1)S(1)} %copy-done, bf16[128,4096]{1,0:T(8,128)(2,1)} %k_hbm.1, bf16[128,4096]{1,0:T(8,128)(2,1)} %v_hbm.1, bf16[128,4096]{1,0:T(8,128)(2,1)} %g_hbm.1, ...), custom_call_target="tpu_custom_call" | custom-call | tf_op jit(solution)/shard_map/pallas_call | solution.py:251
  66.7 1.0 %copy.14 = bf16[128,4096]{1,0:T(8,128)(2,1)} copy(bf16[128,4096]{1,0:T(8,128)(2,1)S(1)} %get-tuple-element.8) | data formatting | bytes 2097152
  67.7 1.0 %copy.15 = bf16[128,4096]{1,0:T(8,128)(2,1)} copy(bf16[128,4096]{1,0:T(8,128)(2,1)S(1)} %get-tuple-element.9) | data formatting | bytes 2097152
  68.6 1.0 %copy.16 = bf16[128,4096]{1,0:T(8,128)(2,1)} copy(bf16[128,4096]{1,0:T(8,128)(2,1)S(1)} %get-tuple-element.10) | data formatting | bytes 2097152
  69.6 1.0 %copy.17 = bf16[128,4096]{1,0:T(8,128)(2,1)} copy(bf16[128,4096]{1,0:T(8,128)(2,1)S(1)} %get-tuple-element.11) | data formatting | bytes 2097152
Async XLA Ops:
  1.4 1.2 %copy-start = (bf16[128,4096]{1,0:T(8,128)(2,1)S(1)}, bf16[128,4096]{1,0:T(8,128)(2,1)}, u32[]{:S(2)}) copy-start(bf16[128,4096]{1,0:T(8,128)(2,1)} %q_hbm.1) | copy-start | bytes 3145732

commit v4 on v3

--- a/solution.py
+++ b/solution.py
@@ -8,7 +8,7 @@
 from jax.sharding import PartitionSpec as P
 
 MESH = pl.DeviceIdType.MESH
-HEADS_PER_CHUNK = 2
+HEADS_PER_CHUNK = 1
 LAG = 2
 GROUPS = 4
 

time: 70.8 us -> 74.8 us (1.056)
  Pallas kernels: 64 us -> 68 us
    pallas_call x1, Pallas kernels: 64 us -> 68 us  [shards(): pl.pallas_call(functools.partial(kernel, n, per), out_shape=[jax.ShapeDty...]
where the time goes in v4:
time: 74.8 us; the launch traced here: 74.6 us
  Pallas kernels  68 us (91%)
  local copies, waits for them, and re-layouts  5.92 us (8%)
    pallas_call x1, Pallas kernels, shards(): pl.pallas_call(functools.partial(kernel, n, per), out_shape=[jax.ShapeDty...  68 us
    unnamed x7, local copies, waits for them, and re-layouts  5.92 us

profile of v4, /device:TPU:0, one launch (start us, length us, event | category | flops | bytes accessed | tf_op | source)
XLA Modules:
  0.0 74.6 jit_solution(12440512780145489875)
XLA Ops:
  0.6 0.8 %copy.9.ld_ref = bf16[128,32]{1,0:T(8,128)(2,1)S(1)} copy(bf16[128,32]{0,1:T(8,128)(2,1)} %param.9) | data formatting | bytes 16384 | tf_op args[4]
  1.4 0.0 copy-start
  1.4 1.2 %copy-done = bf16[128,4096]{1,0:T(8,128)(2,1)S(1)} copy-done((bf16[128,4096]{1,0:T(8,128)(2,1)S(1)}, bf16[128,4096]{1,0:T(8,128)(2,1)}, u32[]{:S(2)}) %copy-start) | copy-done | bytes 1048600
  2.7 68.0 %shard_map.84 = (bf16[128,4096]{1,0:T(8,128)(2,1)S(1)}, bf16[128,4096]{1,0:T(8,128)(2,1)S(1)}, bf16[128,4096]{1,0:T(8,128)(2,1)S(1)}, bf16[128,4096]{1,0:T(8,128)(2,1)S(1)}) custom-call(bf16[128,4096]{1,0:T(8,128)(2,1)S(1)} %copy-done, bf16[128,4096]{1,0:T(8,128)(2,1)} %k_hbm.1, bf16[128,4096]{1,0:T(8,128)(2,1)} %v_hbm.1, bf16[128,4096]{1,0:T(8,128)(2,1)} %g_hbm.1, ...), custom_call_target="tpu_custom_call" | custom-call | tf_op jit(solution)/shard_map/pallas_call | solution.py:251
  70.7 1.0 %copy.14 = bf16[128,4096]{1,0:T(8,128)(2,1)} copy(bf16[128,4096]{1,0:T(8,128)(2,1)S(1)} %get-tuple-element.8) | data formatting | bytes 2097152
  71.6 1.0 %copy.15 = bf16[128,4096]{1,0:T(8,128)(2,1)} copy(bf16[128,4096]{1,0:T(8,128)(2,1)S(1)} %get-tuple-element.9) | data formatting | bytes 2097152
  72.6 1.0 %copy.16 = bf16[128,4096]{1,0:T(8,128)(2,1)} copy(bf16[128,4096]{1,0:T(8,128)(2,1)S(1)} %get-tuple-element.10) | data formatting | bytes 2097152
  73.6 1.0 %copy.17 = bf16[128,4096]{1,0:T(8,128)(2,1)} copy(bf16[128,4096]{1,0:T(8,128)(2,1)S(1)} %get-tuple-element.11) | data formatting | bytes 2097152
Async XLA Ops:
  1.4 1.2 %copy-start = (bf16[128,4096]{1,0:T(8,128)(2,1)S(1)}, bf16[128,4096]{1,0:T(8,128)(2,1)}, u32[]{:S(2)}) copy-start(bf16[128,4096]{1,0:T(8,128)(2,1)} %q_hbm.1) | copy-start | bytes 3145732

commit v5 on v4

--- a/solution.py
+++ b/solution.py
@@ -8,7 +8,7 @@
 from jax.sharding import PartitionSpec as P
 
 MESH = pl.DeviceIdType.MESH
-HEADS_PER_CHUNK = 1
+HEADS_PER_CHUNK = 4
 LAG = 2
 GROUPS = 4
 

time: 74.8 us -> 77.4 us (1.035)
  Pallas kernels: 68 us -> 70.6 us
    pallas_call x1, Pallas kernels: 68 us -> 70.6 us  [shards(): pl.pallas_call(functools.partial(kernel, n, per), out_shape=[jax.ShapeDty...]
where the time goes in v5:
time: 77.4 us; the launch traced here: 77.2 us
  Pallas kernels  70.6 us (91%)
  local copies, waits for them, and re-layouts  5.92 us (8%)
    pallas_call x1, Pallas kernels, shards(): pl.pallas_call(functools.partial(kernel, n, per), out_shape=[jax.ShapeDty...  70.6 us
    unnamed x7, local copies, waits for them, and re-layouts  5.92 us

profile of v5, /device:TPU:0, one launch (start us, length us, event | category | flops | bytes accessed | tf_op | source)
XLA Modules:
  0.0 77.2 jit_solution(1896418929493769865)
XLA Ops:
  0.6 0.8 %copy.9.ld_ref = bf16[128,32]{1,0:T(8,128)(2,1)S(1)} copy(bf16[128,32]{0,1:T(8,128)(2,1)} %param.9) | data formatting | bytes 16384 | tf_op args[4]
  1.4 0.0 copy-start
  1.4 1.2 %copy-done = bf16[128,4096]{1,0:T(8,128)(2,1)S(1)} copy-done((bf16[128,4096]{1,0:T(8,128)(2,1)S(1)}, bf16[128,4096]{1,0:T(8,128)(2,1)}, u32[]{:S(2)}) %copy-start) | copy-done | bytes 1048600
  2.7 70.6 %shard_map.84 = (bf16[128,4096]{1,0:T(8,128)(2,1)S(1)}, bf16[128,4096]{1,0:T(8,128)(2,1)S(1)}, bf16[128,4096]{1,0:T(8,128)(2,1)S(1)}, bf16[128,4096]{1,0:T(8,128)(2,1)S(1)}) custom-call(bf16[128,4096]{1,0:T(8,128)(2,1)S(1)} %copy-done, bf16[128,4096]{1,0:T(8,128)(2,1)} %k_hbm.1, bf16[128,4096]{1,0:T(8,128)(2,1)} %v_hbm.1, bf16[128,4096]{1,0:T(8,128)(2,1)} %g_hbm.1, ...), custom_call_target="tpu_custom_call" | custom-call | tf_op jit(solution)/shard_map/pallas_call | solution.py:251
  73.3 1.0 %copy.14 = bf16[128,4096]{1,0:T(8,128)(2,1)} copy(bf16[128,4096]{1,0:T(8,128)(2,1)S(1)} %get-tuple-element.8) | data formatting | bytes 2097152
  74.3 1.0 %copy.15 = bf16[128,4096]{1,0:T(8,128)(2,1)} copy(bf16[128,4096]{1,0:T(8,128)(2,1)S(1)} %get-tuple-element.9) | data formatting | bytes 2097152
  75.3 1.0 %copy.16 = bf16[128,4096]{1,0:T(8,128)(2,1)} copy(bf16[128,4096]{1,0:T(8,128)(2,1)S(1)} %get-tuple-element.10) | data formatting | bytes 2097152
  76.2 1.0 %copy.17 = bf16[128,4096]{1,0:T(8,128)(2,1)} copy(bf16[128,4096]{1,0:T(8,128)(2,1)S(1)} %get-tuple-element.11) | data formatting | bytes 2097152
Async XLA Ops:
  1.4 1.2 %copy-start = (bf16[128,4096]{1,0:T(8,128)(2,1)S(1)}, bf16[128,4096]{1,0:T(8,128)(2,1)}, u32[]{:S(2)}) copy-start(bf16[128,4096]{1,0:T(8,128)(2,1)} %q_hbm.1) | copy-start | bytes 3145732
